TPU v7x, 32 devices: a whole 2x2x4 slice. The times are simulated.
32 devices in a mesh: groups: 2 (over x), rows: 16 (over z, y, core).
Axes of the slice: x: 2, y: 2, z: 4, core: 2. Of those that a mesh axis runs over, the one named last changes fastest.
Arguments:
- span_inputs: bfloat16 [4096, 8192], P(('groups', 'rows')), parts along dimension 0, may hold values from -6 to 6
- span_outputs: bfloat16 [4096, 8192], P(('groups', 'rows')), parts along dimension 0, may hold values from -6 to 6
- row_counts: int32 [32], P(('groups', 'rows')), parts along dimension 0, may hold values from 1 to 128, 1024 in all
- tile_pairs: int32 [32, 2], P(('groups', 'rows')), parts along dimension 0, may hold values from 0 to 63, as said below
Outputs:
- input_gram: float32 [32, 128, 128], P(('groups', 'rows')), parts along dimension 0
- cross_gram: float32 [32, 128, 128], P(('groups', 'rows')), parts along dimension 0
- target_gram: float32 [32, 128, 128], P(('groups', 'rows')), parts along dimension 0
There are 2 independent parts, one for each index of `groups`. A program takes and returns all parts, laid end to end along the dimension named above; each array names one. Nothing has to cross between parts.
Inputs may be any that keep to these rules, and one draw needn't show every extreme that they name: `row_counts`: the counts sum to 1024. `tile_pairs`: each entry is a block index; in each row the column block lies within 5 of the row block. Tiles may repeat.
All inputs are finite; a program needn't handle non-finite values. No bound on the sum of `row_counts` on one device may be relied on, other than what follows from the above.
Results may differ from a plain program's by a relative error of at most 0.0003.
Values may be sent and summed in bfloat16 or wider, within the bound.
A program may use at most 64 MiB of HBM per device.

v0:
```python
import math

import jax
import jax.numpy as jnp
from jax import lax
from jax.sharding import PartitionSpec as P

D = 8192
BS = 128


def masked_blocks(values, row_counts):
    tok_rows = values.shape[0]
    live_rows = lax.broadcasted_iota(jnp.int32, (tok_rows, 1), 0) < row_counts[0]
    kept = jnp.where(live_rows, values, jnp.zeros_like(values))
    return kept.reshape(tok_rows, D // BS, BS).transpose(1, 0, 2)


def tile_products(left_blocks, right_blocks, target_blocks):
    gram = jnp.einsum("ktb,ktc->kbc", left_blocks, right_blocks, preferred_element_type=jnp.float32)
    cross = jnp.einsum(
        "ktb,ktc->kbc", left_blocks, target_blocks, preferred_element_type=jnp.float32
    )
    square = jnp.einsum(
        "ktb,ktc->kbc", target_blocks, target_blocks, preferred_element_type=jnp.float32
    )
    return (gram, cross, square)


def local(span_inputs, span_outputs, row_counts, tile_pairs):
    input_blocks = masked_blocks(span_inputs, row_counts)
    output_blocks = masked_blocks(span_outputs, row_counts)
    all_pairs = lax.all_gather(tile_pairs, "rows", axis=0, tiled=True)
    row_scale = 1.0 / math.sqrt(lax.axis_size("rows") * span_inputs.shape[0] // 2)
    outgoing = jnp.stack(
        [
            jnp.take(input_blocks, all_pairs[:, 0], axis=0),
            jnp.take(input_blocks, all_pairs[:, 1], axis=0),
            jnp.take(output_blocks, all_pairs[:, 1], axis=0),
        ],
        axis=0,
    )
    arrived = lax.all_to_all(outgoing, "rows", split_axis=1, concat_axis=2, tiled=True)
    input_gram, cross_gram, target_gram = tile_products(arrived[0], arrived[1], arrived[2])
    return (input_gram * row_scale, cross_gram * row_scale, target_gram * row_scale)


def solution(mesh):
    return jax.shard_map(
        local,
        mesh=mesh,
        in_specs=(
            P(("groups", "rows"), None),
            P(("groups", "rows"), None),
            P(("groups", "rows")),
            P(("groups", "rows"), None),
        ),
        out_specs=(
            P(("groups", "rows"), None, None),
            P(("groups", "rows"), None, None),
            P(("groups", "rows"), None, None),
        ),
        check_vma=False,
    )
```

profile of v0, /device:TPU:1, one launch (start us, length us, event | category | flops | bytes accessed | tf_op | source)
XLA Modules:
  0.0 91.2 jit_solution(1270049055361909091)
XLA Ops:
  0.6 23.0 %all-gather = s32[16,1,2]{2,1,0:T(1,128)S(1)} all-gather(s32[1,1,2]{2,1,0:T(1,128)} %bitcast.67), channel_id=1, replica_groups=mesh['groups'=2,'rows'=16] {'rows'}, dimensions={0}, use_global_device_ids=true | all-gather | bytes 136 | tf_op jit(solution)/shard_map/all_gather | solution.py:33
  23.6 0.1 copy.23
  23.8 0.0 copy-start
  23.8 4.2 %copy.24 = bf16[128,8192]{0,1:T(8,128)(2,1)} copy(bf16[128,8192]{1,0:T(8,128)(2,1)} %param.6) | data formatting | bytes 4194304 | tf_op args[0]
  28.0 0.0 copy-done
  28.0 2.4 %copy.26 = bf16[128,8192]{0,1:T(8,128)(2,1)} copy(bf16[128,8192]{1,0:T(8,128)(2,1)S(1)} %copy-done) | data formatting | bytes 4194304 | tf_op args[1]
  31.1 3.8 %broadcast_select_fusion.1 = (bf16[128,8192]{0,1:T(8,128)(2,1)}, bf16[128,8192]{0,1:T(8,128)(2,1)S(1)}) fusion(bf16[128,8192]{0,1:T(8,128)(2,1)} %copy.24, pred[128]{0:T(512)(128)(4,1)S(1)} %iota_compare_fusion, bf16[128,8192]{0,1:T(8,128)(2,1)} %copy.26), kind=kLoop, calls=%fused_computation.4 | loop fusion | flops 2097152 | bytes 8388736 | tf_op jit(solution)/shard_map/jit(_where)/select_n | solution.py:15
  34.9 4.1 %copy.25 = bf16[128,64,128]{2,0,1:T(8,128)(2,1)} copy(bf16[128,64,128]{0,2,1:T(8,128)(2,1)} %bitcast.62) | data formatting | bytes 4194304 | tf_op jit(solution)/shard_map/reshape | solution.py:16
  39.0 2.2 %gather_fusion.1 = bf16[16,128,128]{2,1,0:T(8,128)(2,1)S(1)} fusion(bf16[64,128,128]{2,1,0:T(8,128)(2,1)} %bitcast.63, s32[1024]{0:T(1024)S(1)} %pad_clamp_fusion), kind=kCustom, calls=%fused_computation.1.clone | custom fusion | bytes 1048640 | tf_op jit(solution)/shard_map/jit(_take)/gather | solution.py:38
  41.2 2.2 %gather_fusion = bf16[16,128,128]{2,1,0:T(8,128)(2,1)S(1)} fusion(bf16[64,128,128]{2,1,0:T(8,128)(2,1)} %bitcast.64, s32[1024]{0:T(1024)S(1)} %pad_clamp_fusion.1), kind=kCustom, calls=%fused_computation.clone | custom fusion | bytes 1048640 | tf_op jit(solution)/shard_map/jit(_take)/gather | solution.py:37
  43.4 2.9 %copy.27 = bf16[128,64,128]{2,0,1:T(8,128)(2,1)} copy(bf16[128,64,128]{0,2,1:T(8,128)(2,1)S(1)} %bitcast.61) | data formatting | bytes 4194304 | tf_op jit(solution)/shard_map/reshape | solution.py:16
  46.3 2.2 %gather_fusion.2 = bf16[16,128,128]{2,1,0:T(8,128)(2,1)S(1)} fusion(bf16[64,128,128]{2,1,0:T(8,128)(2,1)} %bitcast.65, s32[1024]{0:T(1024)S(1)} %pad_clamp_fusion), kind=kCustom, calls=%fused_computation.2.clone | custom fusion | bytes 1048640 | tf_op jit(solution)/shard_map/jit(_take)/gather | solution.py:39
  48.6 0.2 select_bitcast_fusion.1
  48.8 0.2 pad_maximum_fusion
  49.0 0.2 copy.28
  49.2 39.1 %all_to_all.4 = bf16[3,16,128,128]{3,2,0,1:T(8,128)(2,1)S(1)} all-to-all(bf16[3,16,128,128]{3,2,0,1:T(8,128)(2,1)S(1)} %copy.28), channel_id=1, replica_groups=mesh['groups'=2,'rows'=16] {'rows'}, dimensions={1} | all-to-all | bytes 3145728 | tf_op jit(solution)/shard_map/all_to_all | solution.py:43
  88.3 1.0 %fusion.1 = f32[1,128,128]{2,1,0:T(8,128)} fusion(bf16[3,16,128,128]{3,2,0,1:T(8,128)(2,1)S(1)} %all_to_all.4), kind=kOutput, calls=%fused_computation.8 | convolution fusion | flops 67125248 | bytes 589824 | tf_op jit(solution)/shard_map/ktb,ktc->kbc/dot_general | solution.py:24
  89.3 1.0 %fusion.3 = f32[1,128,128]{2,1,0:T(8,128)} fusion(bf16[3,16,128,128]{3,2,0,1:T(8,128)(2,1)S(1)} %all_to_all.4), kind=kOutput, calls=%fused_computation.11 | convolution fusion | flops 67125248 | bytes 1114112 | tf_op jit(solution)/shard_map/ktb,ktc->kbc/dot_general | solution.py:21
  90.2 1.0 %fusion.5 = f32[1,128,128]{2,1,0:T(8,128)} fusion(bf16[3,16,128,128]{3,2,0,1:T(8,128)(2,1)S(1)} %all_to_all.4), kind=kOutput, calls=%fused_computation.14 | convolution fusion | flops 67125248 | bytes 1114112 | tf_op jit(solution)/shard_map/ktb,ktc->kbc/dot_general | solution.py:20
  (4 shorter events, 0.0 us)
Async XLA Ops:
  23.8 4.2 %copy-start = (bf16[128,8192]{1,0:T(8,128)(2,1)S(1)}, bf16[128,8192]{1,0:T(8,128)(2,1)}, u32[]{:S(2)}) copy-start(bf16[128,8192]{1,0:T(8,128)(2,1)} %param.7) | copy-start | bytes 6291460
where the time goes:
time: 91.6 us; the launch traced here: 91.2 us
  blocking collectives  62.2 us (68%)
  local copies, waits for them, and re-layouts  20.6 us (22%)
  other arithmetic  4.22 us (5%)
  matrix products  2.91 us (3%)
  between operations  1.36 us (1%)
    all_to_all x1, blocking collectives, local(): lax.all_to_all(outgoing, 'rows', split_axis=1, concat_axis=2, tiled=True)  39.1 us
    all_gather x1, blocking collectives, local(): all_pairs = lax.all_gather(tile_pairs, 'rows', axis=0, tiled=True)  23 us
    reshape x2, local copies, waits for them, and re-layouts, masked_blocks(): return kept.reshape(tok_rows, D // BS, BS).transpose(1, 0, 2)  6.96 us
    unnamed x4, local copies, waits for them, and re-layouts  6.65 us
    select_n x1, other arithmetic, masked_blocks(): kept = jnp.where(live_rows, values, jnp.zeros_like(values))  3.81 us
    gather x1, local copies, waits for them, and re-layouts, local(): jnp.take(input_blocks, all_pairs[:, 0], axis=0)  2.24 us
    gather x1, local copies, waits for them, and re-layouts, local(): jnp.take(output_blocks, all_pairs[:, 1], axis=0)  2.24 us
    gather x1, local copies, waits for them, and re-layouts, local(): jnp.take(input_blocks, all_pairs[:, 1], axis=0)  2.24 us

commit v1 on v0

v1 whole, which is shorter than its diff:
```python
import functools
import math

import jax
import jax.numpy as jnp
from jax import lax
from jax.experimental import pallas as pl
from jax.experimental.pallas import tpu as pltpu
from jax.sharding import PartitionSpec as P

BS = 128
CLUSTER = 4


def contract_rows(left, right):
    return lax.dot_general(left, right, (((0,), (0,)), ((), ())), preferred_element_type=jnp.float32)


def gram_kernel(
    n, scale, in_hbm, out_hbm, counts, pairs, gram_ref, cross_ref, target_ref,
    in_v, out_v, all_pairs, stage, arrived, partial, from_left, from_right,
    load_sem, pair_send, pair_recv, raw_send, raw_recv, right_send, right_recv, left_send, left_recv,
):
    span = n // CLUSTER
    me = lax.axis_index("rows")
    z = me // CLUSTER
    q = me % CLUSTER

    barrier = pltpu.get_barrier_semaphore()

    @pl.loop(1, n)
    def _(step):
        pl.semaphore_signal(
            barrier, inc=1, device_id={"rows": (me + step) % n}, device_id_type=pl.DeviceIdType.MESH
        )

    @pl.loop(0, in_v.shape[0])
    def _(b):
        columns = pl.ds(pl.multiple_of(b * BS, BS), BS)
        pltpu.make_async_copy(in_hbm.at[:, columns], in_v.at[b], load_sem.at[0]).start()
        pltpu.make_async_copy(out_hbm.at[:, columns], out_v.at[b], load_sem.at[1]).start()

    pl.semaphore_wait(barrier, n - 1)

    def pair_copy(peer, slot):
        return pltpu.make_async_remote_copy(
            src_ref=pairs, dst_ref=all_pairs.at[slot], send_sem=pair_send.at[peer],
            recv_sem=pair_recv.at[slot], device_id={"rows": peer}, device_id_type=pl.DeviceIdType.MESH,
        )

    @pl.loop(1, n)
    def _(step):
        pair_copy((me + step) % n, me).start()

    all_pairs[me, 0, 0] = pairs[0, 0]
    all_pairs[me, 0, 1] = pairs[0, 1]
    rows = in_v.shape[1]
    live = lax.broadcasted_iota(jnp.int32, (rows, BS), 0) < counts[0]
    pltpu.make_async_copy(in_v, in_v, load_sem.at[0]).wait()
    pltpu.make_async_copy(out_v, out_v, load_sem.at[1]).wait()

    @pl.loop(1, n)
    def _(step):
        peer = (me + step) % n
        pair_copy(peer, peer).wait_recv()

    def block(values, index):
        picked = values[index]
        return jnp.where(live, picked, jnp.zeros_like(picked))

    def blocks(k):
        row_block = all_pairs[k, 0, 0]
        col_block = all_pairs[k, 0, 1]
        return block(in_v, row_block), block(in_v, col_block), block(out_v, col_block)

    def raw_copy(t, dest, source):
        return pltpu.make_async_remote_copy(
            src_ref=stage.at[t * CLUSTER + dest], dst_ref=arrived.at[t, :, source],
            send_sem=raw_send.at[t * CLUSTER + dest], recv_sem=raw_recv.at[t * CLUSTER + source],
            device_id={"rows": z * CLUSTER + dest}, device_id_type=pl.DeviceIdType.MESH,
        )

    def right_copy(t):
        return pltpu.make_async_remote_copy(
            src_ref=partial.at[t], dst_ref=from_left.at[t], send_sem=right_send.at[t],
            recv_sem=right_recv.at[t], device_id={"rows": (me + CLUSTER) % n},
            device_id_type=pl.DeviceIdType.MESH,
        )

    def left_copy(t):
        return pltpu.make_async_remote_copy(
            src_ref=partial.at[t], dst_ref=from_right.at[t], send_sem=left_send.at[t],
            recv_sem=left_recv.at[t], device_id={"rows": (me + n - CLUSTER) % n},
            device_id_type=pl.DeviceIdType.MESH,
        )

    def send_raw(t):
        for offset in (2, 1, 3):
            dest = (q + offset) % CLUSTER
            k = t * CLUSTER + dest
            for i, values in enumerate(blocks(k)):
                stage[k, i] = values
            raw_copy(t, dest, q).start()
        for i, values in enumerate(blocks(t * CLUSTER + q)):
            arrived[t, i, q] = values

    def products(t):
        for offset in (2, 1, 3):
            source = (q + offset) % CLUSTER
            raw_copy(t, source, source).wait_recv()
        left = arrived[t, 0].reshape(CLUSTER * rows, BS)
        right = arrived[t, 1].reshape(CLUSTER * rows, BS)
        target = arrived[t, 2].reshape(CLUSTER * rows, BS)
        return (
            contract_rows(left, right), contract_rows(left, target), contract_rows(target, target)
        )

    @pl.loop(0, span - 1)
    def _(j):
        @pl.when(span - 1 - j > z)
        def _():
            send_raw(span - 1 - j)

        @pl.when(j < z)
        def _():
            send_raw(j)

    send_raw(z)

    def store_partial(t):
        for i, values in enumerate(products(t)):
            partial[t, i] = values

    @pl.loop(0, span - 1)
    def _(j):
        @pl.when(span - 1 - j > z)
        def _():
            t = span - 1 - j
            store_partial(t)

            @pl.when(z > 0)
            def _():
                right_copy(t).wait_recv()
                partial[t] = partial[t] + from_left[t]

            right_copy(t).start()

        @pl.when(j < z)
        def _():
            store_partial(j)

            @pl.when(z < span - 1)
            def _():
                left_copy(j).wait_recv()
                partial[j] = partial[j] + from_right[j]

            left_copy(j).start()

    store_partial(z)

    @pl.when(z > 0)
    def _():
        right_copy(z).wait_recv()
        partial[z] = partial[z] + from_left[z]

    @pl.when(z < span - 1)
    def _():
        left_copy(z).wait_recv()
        partial[z] = partial[z] + from_right[z]

    gram_ref[0] = partial[z, 0] * scale
    cross_ref[0] = partial[z, 1] * scale
    target_ref[0] = partial[z, 2] * scale

    @pl.loop(1, n)
    def _(step):
        pair_copy((me + step) % n, me).wait_send()

    @pl.loop(0, span)
    def _(t):
        for offset in (2, 1, 3):
            raw_copy(t, (q + offset) % CLUSTER, q).wait_send()

        @pl.when(t > z)
        def _():
            right_copy(t).wait_send()

        @pl.when(t < z)
        def _():
            left_copy(t).wait_send()


def local(span_inputs, span_outputs, row_counts, tile_pairs):
    n = lax.axis_size("rows")
    rows, width = span_inputs.shape
    scale = 1.0 / math.sqrt(n * rows // 2)
    span = n // CLUSTER
    half, full = span_inputs.dtype, jnp.float32
    tile = jax.ShapeDtypeStruct((1, BS, BS), full)
    scratch = 2 * (2 * rows * width + 2 * n * 3 * rows * BS) + 4 * 3 * span * 3 * BS * BS
    dma = pltpu.SemaphoreType.DMA
    return pl.pallas_call(
        functools.partial(gram_kernel, n, scale),
        out_shape=(tile, tile, tile),
        in_specs=[
            pl.BlockSpec(memory_space=pl.ANY),
            pl.BlockSpec(memory_space=pl.ANY),
            pl.BlockSpec(memory_space=pltpu.SMEM),
            pl.BlockSpec(memory_space=pltpu.SMEM),
        ],
        out_specs=[pl.BlockSpec(memory_space=pltpu.VMEM)] * 3,
        scratch_shapes=[
            pltpu.VMEM((width // BS, rows, BS), half),
            pltpu.VMEM((width // BS, rows, BS), half),
            pltpu.SMEM((n, 1, 2), jnp.int32),
            pltpu.VMEM((n, 3, rows, BS), half),
            pltpu.VMEM((span, 3, CLUSTER, rows, BS), half),
            pltpu.VMEM((span, 3, BS, BS), full),
            pltpu.VMEM((span, 3, BS, BS), full),
            pltpu.VMEM((span, 3, BS, BS), full),
            dma((2,)), dma((n,)), dma((n,)), dma((n,)), dma((n,)),
            dma((span,)), dma((span,)), dma((span,)), dma((span,)),
        ],
        compiler_params=pltpu.CompilerParams(
            collective_id=0, has_side_effects=True, vmem_limit_bytes=scratch + 6 * 2**20
        ),
    )(span_inputs, span_outputs, row_counts, tile_pairs)


def solution(mesh):
    rows = P(("groups", "rows"))
    return jax.shard_map(
        local, mesh=mesh, in_specs=(rows, rows, rows, rows), out_specs=(rows, rows, rows), check_vma=False
    )
```

time: 91.6 us -> 47.7 us (0.52)
  the two profiles are of different devices: /device:TPU:1 before, /device:TPU:0 now
where the time goes in v1:
time: 47.7 us; the launch traced here: 47.5 us
  Pallas kernels  40.5 us (85%)
  local copies, waits for them, and re-layouts  5.72 us (12%)
  between operations  1.3 us (3%)
    pallas_call x1, Pallas kernels, local(): pl.pallas_call(functools.partial(gram_kernel, n, scale), out_shape=(tile,...  40.5 us
    unnamed x9, local copies, waits for them, and re-layouts  5.72 us

profile of v1, /device:TPU:0, one launch (start us, length us, event | category | flops | bytes accessed | tf_op | source)
XLA Modules:
  0.0 47.5 jit_solution(2693519998428673164)
XLA Ops:
  1.3 0.0 copy-start
  1.3 1.6 %copy-done = bf16[128,8192]{1,0:T(8,128)(2,1)S(1)} copy-done((bf16[128,8192]{1,0:T(8,128)(2,1)S(1)}, bf16[128,8192]{1,0:T(8,128)(2,1)}, u32[]{:S(2)}) %copy-start) | copy-done | bytes 2097176
  2.9 0.0 copy-start.1
  2.9 1.6 %copy-done.1 = bf16[128,8192]{1,0:T(8,128)(2,1)S(1)} copy-done((bf16[128,8192]{1,0:T(8,128)(2,1)S(1)}, bf16[128,8192]{1,0:T(8,128)(2,1)}, u32[]{:S(2)}) %copy-start.1) | copy-done | bytes 2097176
  4.5 0.0 copy-start.2
  4.5 0.7 %copy-done.2 = s32[1,2]{1,0:T(1,128)S(1)} copy-done((s32[1,2]{1,0:T(1,128)S(1)}, s32[1,2]{1,0:T(1,128)}, u32[]{:S(2)}) %copy-start.2) | copy-done | bytes 32
  5.1 40.5 %shard_map.67 = (f32[1,128,128]{2,1,0:T(8,128)S(1)}, f32[1,128,128]{2,1,0:T(8,128)S(1)}, f32[1,128,128]{2,1,0:T(8,128)S(1)}) custom-call(bf16[128,8192]{1,0:T(8,128)(2,1)S(1)} %copy-done, bf16[128,8192]{1,0:T(8,128)(2,1)S(1)} %copy-done.1, s32[1]{0:T(128)S(6)} %copy.10.counts, s32[1,2]{1,0:T(1,128)S(1)} %copy-done.2), custom_call_target="tpu_custom_call" | custom-call | tf_op jit(solution)/shard_map/pallas_call | solution.py:202
  45.6 0.6 %copy.11 = f32[1,128,128]{2,1,0:T(8,128)} copy(f32[1,128,128]{2,1,0:T(8,128)S(1)} %get-tuple-element.6) | data formatting | bytes 131072
  46.2 0.6 %copy.12 = f32[1,128,128]{2,1,0:T(8,128)} copy(f32[1,128,128]{2,1,0:T(8,128)S(1)} %get-tuple-element.7) | data formatting | bytes 131072
  46.9 0.6 %copy.13 = f32[1,128,128]{2,1,0:T(8,128)} copy(f32[1,128,128]{2,1,0:T(8,128)S(1)} %get-tuple-element.8) | data formatting | bytes 131072
Async XLA Ops:
  1.3 1.6 %copy-start = (bf16[128,8192]{1,0:T(8,128)(2,1)S(1)}, bf16[128,8192]{1,0:T(8,128)(2,1)}, u32[]{:S(2)}) copy-start(bf16[128,8192]{1,0:T(8,128)(2,1)} %in_hbm.1) | copy-start | bytes 6291460
  2.9 1.6 %copy-start.1 = (bf16[128,8192]{1,0:T(8,128)(2,1)S(1)}, bf16[128,8192]{1,0:T(8,128)(2,1)}, u32[]{:S(2)}) copy-start(bf16[128,8192]{1,0:T(8,128)(2,1)} %out_hbm.1) | copy-start | bytes 6291460
  4.5 0.7 %copy-start.2 = (s32[1,2]{1,0:T(1,128)S(1)}, s32[1,2]{1,0:T(1,128)}, u32[]{:S(2)}) copy-start(s32[1,2]{1,0:T(1,128)} %pairs.1) | copy-start | bytes 28

commit v2 on v1

--- a/solution.py
+++ b/solution.py
@@ -10,6 +10,8 @@
 
 BS = 128
 CLUSTER = 4
+AHEAD = 2
+PARTS = 3
 
 
 def contract_rows(left, right):
@@ -17,7 +19,7 @@
 
 
 def gram_kernel(
-    n, scale, in_hbm, out_hbm, counts, pairs, gram_ref, cross_ref, target_ref,
+    n, in_hbm, out_hbm, counts, pairs, sums_ref,
     in_v, out_v, all_pairs, stage, arrived, partial, from_left, from_right,
     load_sem, pair_send, pair_recv, raw_send, raw_recv, right_send, right_recv, left_send, left_recv,
 ):
@@ -80,17 +82,17 @@
             device_id={"rows": z * CLUSTER + dest}, device_id_type=pl.DeviceIdType.MESH,
         )
 
-    def right_copy(t):
-        return pltpu.make_async_remote_copy(
-            src_ref=partial.at[t], dst_ref=from_left.at[t], send_sem=right_send.at[t],
-            recv_sem=right_recv.at[t], device_id={"rows": (me + CLUSTER) % n},
+    def right_copy(t, i):
+        return pltpu.make_async_remote_copy(
+            src_ref=partial.at[t, i], dst_ref=from_left.at[t, i], send_sem=right_send.at[t, i],
+            recv_sem=right_recv.at[t, i], device_id={"rows": (me + CLUSTER) % n},
             device_id_type=pl.DeviceIdType.MESH,
         )
 
-    def left_copy(t):
-        return pltpu.make_async_remote_copy(
-            src_ref=partial.at[t], dst_ref=from_right.at[t], send_sem=left_send.at[t],
-            recv_sem=left_recv.at[t], device_id={"rows": (me + n - CLUSTER) % n},
+    def left_copy(t, i):
+        return pltpu.make_async_remote_copy(
+            src_ref=partial.at[t, i], dst_ref=from_right.at[t, i], send_sem=left_send.at[t, i],
+            recv_sem=left_recv.at[t, i], device_id={"rows": (me + n - CLUSTER) % n},
             device_id_type=pl.DeviceIdType.MESH,
         )
 
@@ -105,9 +107,6 @@
             arrived[t, i, q] = values
 
     def products(t):
-        for offset in (2, 1, 3):
-            source = (q + offset) % CLUSTER
-            raw_copy(t, source, source).wait_recv()
         left = arrived[t, 0].reshape(CLUSTER * rows, BS)
         right = arrived[t, 1].reshape(CLUSTER * rows, BS)
         target = arrived[t, 2].reshape(CLUSTER * rows, BS)
@@ -115,62 +114,55 @@
             contract_rows(left, right), contract_rows(left, target), contract_rows(target, target)
         )
 
-    @pl.loop(0, span - 1)
-    def _(j):
-        @pl.when(span - 1 - j > z)
+    def tile_of(slot):
+        right, left = span - 1 - z, z
+        both = jnp.minimum(right, left)
+        turn = slot // 2
+        upper = (z >= span // 2).astype(jnp.int32)
+        goes_left = (slot + upper) % 2
+        paired = jnp.where(goes_left == 1, turn, span - 1 - turn)
+        single = jnp.where(right > left, span - 1 - (slot - both), slot - both)
+        t = jnp.where(slot < 2 * both, paired, single)
+        return jnp.where(slot == span - 1, z, t)
+
+    @pl.loop(0, AHEAD)
+    def _(slot):
+        send_raw(tile_of(slot))
+
+    @pl.loop(0, span)
+    def _(slot):
+        t = tile_of(slot)
+        for offset in (2, 1, 3):
+            source = (q + offset) % CLUSTER
+            raw_copy(t, source, source).wait_recv()
+
+        @pl.when(slot + AHEAD < span)
         def _():
-            send_raw(span - 1 - j)
-
-        @pl.when(j < z)
-        def _():
-            send_raw(j)
-
-    send_raw(z)
-
-    def store_partial(t):
+            send_raw(tile_of(slot + AHEAD))
+
         for i, values in enumerate(products(t)):
             partial[t, i] = values
 
-    @pl.loop(0, span - 1)
-    def _(j):
-        @pl.when(span - 1 - j > z)
-        def _():
-            t = span - 1 - j
-            store_partial(t)
-
-            @pl.when(z > 0)
-            def _():
-                right_copy(t).wait_recv()
-                partial[t] = partial[t] + from_left[t]
-
-            right_copy(t).start()
-
-        @pl.when(j < z)
-        def _():
-            store_partial(j)
-
-            @pl.when(z < span - 1)
-            def _():
-                left_copy(j).wait_recv()
-                partial[j] = partial[j] + from_right[j]
-
-            left_copy(j).start()
-
-    store_partial(z)
-
-    @pl.when(z > 0)
-    def _():
-        right_copy(z).wait_recv()
-        partial[z] = partial[z] + from_left[z]
-
-    @pl.when(z < span - 1)
-    def _():
-        left_copy(z).wait_recv()
-        partial[z] = partial[z] + from_right[z]
-
-    gram_ref[0] = partial[z, 0] * scale
-    cross_ref[0] = partial[z, 1] * scale
-    target_ref[0] = partial[z, 2] * scale
+        for i in range(PARTS):
+            @pl.when((z > 0) & (t >= z))
+            def _():
+                right_copy(t, i).wait_recv()
+                partial[t, i] = partial[t, i] + from_left[t, i]
+
+            @pl.when((z < span - 1) & (t <= z))
+            def _():
+                left_copy(t, i).wait_recv()
+                partial[t, i] = partial[t, i] + from_right[t, i]
+
+            @pl.when(t > z)
+            def _():
+                right_copy(t, i).start()
+
+            @pl.when(t < z)
+            def _():
+                left_copy(t, i).start()
+
+    sums_ref[...] = partial[z]
 
     @pl.loop(1, n)
     def _(step):
@@ -181,13 +173,14 @@
         for offset in (2, 1, 3):
             raw_copy(t, (q + offset) % CLUSTER, q).wait_send()
 
-        @pl.when(t > z)
-        def _():
-            right_copy(t).wait_send()
-
-        @pl.when(t < z)
-        def _():
-            left_copy(t).wait_send()
+        for i in range(PARTS):
+            @pl.when(t > z)
+            def _():
+                right_copy(t, i).wait_send()
+
+            @pl.when(t < z)
+            def _():
+                left_copy(t, i).wait_send()
 
 
 def local(span_inputs, span_outputs, row_counts, tile_pairs):
@@ -196,19 +189,18 @@
     scale = 1.0 / math.sqrt(n * rows // 2)
     span = n // CLUSTER
     half, full = span_inputs.dtype, jnp.float32
-    tile = jax.ShapeDtypeStruct((1, BS, BS), full)
     scratch = 2 * (2 * rows * width + 2 * n * 3 * rows * BS) + 4 * 3 * span * 3 * BS * BS
     dma = pltpu.SemaphoreType.DMA
-    return pl.pallas_call(
-        functools.partial(gram_kernel, n, scale),
-        out_shape=(tile, tile, tile),
+    sums = pl.pallas_call(
+        functools.partial(gram_kernel, n),
+        out_shape=jax.ShapeDtypeStruct((3, BS, BS), full),
         in_specs=[
             pl.BlockSpec(memory_space=pl.ANY),
             pl.BlockSpec(memory_space=pl.ANY),
             pl.BlockSpec(memory_space=pltpu.SMEM),
             pl.BlockSpec(memory_space=pltpu.SMEM),
         ],
-        out_specs=[pl.BlockSpec(memory_space=pltpu.VMEM)] * 3,
+        out_specs=pl.BlockSpec(memory_space=pltpu.VMEM),
         scratch_shapes=[
             pltpu.VMEM((width // BS, rows, BS), half),
             pltpu.VMEM((width // BS, rows, BS), half),
@@ -219,12 +211,13 @@
             pltpu.VMEM((span, 3, BS, BS), full),
             pltpu.VMEM((span, 3, BS, BS), full),
             dma((2,)), dma((n,)), dma((n,)), dma((n,)), dma((n,)),
-            dma((span,)), dma((span,)), dma((span,)), dma((span,)),
+            *[dma((span, PARTS))] * 4,
         ],
         compiler_params=pltpu.CompilerParams(
-            collective_id=0, has_side_effects=True, vmem_limit_bytes=scratch + 6 * 2**20
+            collective_id=0, has_side_effects=True, vmem_limit_bytes=60 * 2**20
         ),
     )(span_inputs, span_outputs, row_counts, tile_pairs)
+    return (sums[0:1] * scale, sums[1:2] * scale, sums[2:3] * scale)
 
 
 def solution(mesh):

time: 47.7 us -> 35.3 us (0.74)
  the two profiles are of different devices: /device:TPU:0 before, /device:TPU:19 now
where the time goes in v2:
time: 35.3 us; the launch traced here: 35.1 us
  Pallas kernels  32.2 us (91%)
  other arithmetic  1.58 us (4%)
  between operations  1.28 us (4%)
    pallas_call x1, Pallas kernels, local(): pl.pallas_call(functools.partial(gram_kernel, n), out_shape=jax.ShapeDtyp...  32.2 us
    mul x1, other arithmetic, local(): return (sums[0:1] * scale, sums[1:2] * scale, sums[2:3] * scale)  1.58 us

profile of v2, /device:TPU:19, one launch (start us, length us, event | category | flops | bytes accessed | tf_op | source)
XLA Modules:
  0.0 35.1 jit_solution(15827689959389144252)
XLA Ops:
  1.3 32.2 %shard_map.67 = f32[3,128,128]{2,1,0:T(8,128)} custom-call(bf16[128,8192]{1,0:T(8,128)(2,1)} %in_hbm.1, bf16[128,8192]{1,0:T(8,128)(2,1)} %out_hbm.1, s32[1]{0:T(128)S(6)} %copy.7.counts, s32[1,2]{1,0:T(1,128)} %pairs.1), custom_call_target="tpu_custom_call" | custom-call | tf_op jit(solution)/shard_map/pallas_call | solution.py:194
  33.5 1.6 %slice_multiply_fusion = (f32[1,128,128]{2,1,0:T(8,128)}, f32[1,128,128]{2,1,0:T(8,128)}, f32[1,128,128]{2,1,0:T(8,128)}) fusion(f32[3,128,128]{2,1,0:T(8,128)} %shard_map.67), kind=kLoop, calls=%fused_computation | loop fusion | flops 49152 | bytes 393216 | tf_op jit(solution)/shard_map/mul | solution.py:220

commit v3 on v2

--- a/solution.py
+++ b/solution.py
@@ -19,14 +19,20 @@
 
 
 def gram_kernel(
-    n, in_hbm, out_hbm, counts, pairs, sums_ref,
-    in_v, out_v, all_pairs, stage, arrived, partial, from_left, from_right,
+    n, in_hbm, out_hbm, counts_hbm, pairs_hbm, sums_ref,
+    in_v, out_v, counts, pairs, all_pairs, stage, arrived, partial, from_left, from_right,
     load_sem, pair_send, pair_recv, raw_send, raw_recv, right_send, right_recv, left_send, left_recv,
 ):
     span = n // CLUSTER
     me = lax.axis_index("rows")
     z = me // CLUSTER
     q = me % CLUSTER
+    crossing = 3 - 2 * (me % 2)
+
+    load_pairs = pltpu.make_async_copy(pairs_hbm, pairs, load_sem.at[2])
+    load_counts = pltpu.make_async_copy(counts_hbm, counts, load_sem.at[3])
+    load_pairs.start()
+    load_counts.start()
 
     barrier = pltpu.get_barrier_semaphore()
 
@@ -42,6 +48,8 @@
         pltpu.make_async_copy(in_hbm.at[:, columns], in_v.at[b], load_sem.at[0]).start()
         pltpu.make_async_copy(out_hbm.at[:, columns], out_v.at[b], load_sem.at[1]).start()
 
+    load_pairs.wait()
+    load_counts.wait()
     pl.semaphore_wait(barrier, n - 1)
 
     def pair_copy(peer, slot):
@@ -50,29 +58,26 @@
             recv_sem=pair_recv.at[slot], device_id={"rows": peer}, device_id_type=pl.DeviceIdType.MESH,
         )
 
+    turn = jnp.where(z < span // 2, n - 1, 1)
+
     @pl.loop(1, n)
     def _(step):
-        pair_copy((me + step) % n, me).start()
-
-    all_pairs[me, 0, 0] = pairs[0, 0]
-    all_pairs[me, 0, 1] = pairs[0, 1]
+        pair_copy((me + step * turn) % n, me).start()
+
+    all_pairs[me, 0] = pairs[0]
+    all_pairs[me, 1] = pairs[1]
     rows = in_v.shape[1]
     live = lax.broadcasted_iota(jnp.int32, (rows, BS), 0) < counts[0]
     pltpu.make_async_copy(in_v, in_v, load_sem.at[0]).wait()
     pltpu.make_async_copy(out_v, out_v, load_sem.at[1]).wait()
 
-    @pl.loop(1, n)
-    def _(step):
-        peer = (me + step) % n
-        pair_copy(peer, peer).wait_recv()
-
     def block(values, index):
         picked = values[index]
         return jnp.where(live, picked, jnp.zeros_like(picked))
 
     def blocks(k):
-        row_block = all_pairs[k, 0, 0]
-        col_block = all_pairs[k, 0, 1]
+        row_block = all_pairs[k, 0]
+        col_block = all_pairs[k, 1]
         return block(in_v, row_block), block(in_v, col_block), block(out_v, col_block)
 
     def raw_copy(t, dest, source):
@@ -97,7 +102,14 @@
         )
 
     def send_raw(t):
-        for offset in (2, 1, 3):
+        for source in range(CLUSTER):
+            k = t * CLUSTER + source
+
+            @pl.when(k != me)
+            def _():
+                pair_copy(k, k).wait_recv()
+
+        for offset in (2, crossing, CLUSTER - crossing):
             dest = (q + offset) % CLUSTER
             k = t * CLUSTER + dest
             for i, values in enumerate(blocks(k)):
@@ -197,26 +209,28 @@
         in_specs=[
             pl.BlockSpec(memory_space=pl.ANY),
             pl.BlockSpec(memory_space=pl.ANY),
-            pl.BlockSpec(memory_space=pltpu.SMEM),
-            pl.BlockSpec(memory_space=pltpu.SMEM),
+            pl.BlockSpec(memory_space=pl.ANY),
+            pl.BlockSpec(memory_space=pl.ANY),
         ],
         out_specs=pl.BlockSpec(memory_space=pltpu.VMEM),
         scratch_shapes=[
             pltpu.VMEM((width // BS, rows, BS), half),
             pltpu.VMEM((width // BS, rows, BS), half),
-            pltpu.SMEM((n, 1, 2), jnp.int32),
+            pltpu.SMEM((1,), jnp.int32),
+            pltpu.SMEM((2,), jnp.int32),
+            pltpu.SMEM((n, 2), jnp.int32),
             pltpu.VMEM((n, 3, rows, BS), half),
             pltpu.VMEM((span, 3, CLUSTER, rows, BS), half),
             pltpu.VMEM((span, 3, BS, BS), full),
             pltpu.VMEM((span, 3, BS, BS), full),
             pltpu.VMEM((span, 3, BS, BS), full),
-            dma((2,)), dma((n,)), dma((n,)), dma((n,)), dma((n,)),
+            dma((4,)), dma((n,)), dma((n,)), dma((n,)), dma((n,)),
             *[dma((span, PARTS))] * 4,
         ],
         compiler_params=pltpu.CompilerParams(
-            collective_id=0, has_side_effects=True, vmem_limit_bytes=60 * 2**20
+            collective_id=0, has_side_effects=True, vmem_limit_bytes=53 * 2**20
         ),
-    )(span_inputs, span_outputs, row_counts, tile_pairs)
+    )(span_inputs, span_outputs, row_counts, tile_pairs.reshape(2))
     return (sums[0:1] * scale, sums[1:2] * scale, sums[2:3] * scale)
 
 

time: 35.3 us -> 33.4 us (0.946)
  Pallas kernels: 32.2 us -> 30.6 us
  other arithmetic: 1.58 us -> 0.68 us
  local copies, waits for them, and re-layouts: 0 us -> 0.65 us
    pallas_call x1, Pallas kernels: 32.2 us -> 30.6 us  [local(): pl.pallas_call(functools.partial(gram_kernel, n), out_shape=jax.ShapeDtyp...]
    mul x1, other arithmetic: 1.58 us -> 0.68 us  [local(): return (sums[0:1] * scale, sums[1:2] * scale, sums[2:3] * scale)]
    unnamed x0 -> x2, local copies, waits for them, and re-layouts: none -> 0.65 us
where the time goes in v3:
time: 33.4 us; the launch traced here: 33.2 us
  Pallas kernels  30.6 us (92%)
  between operations  1.29 us (4%)
  other arithmetic  0.68 us (2%)
  local copies, waits for them, and re-layouts  0.65 us (2%)
    pallas_call x1, Pallas kernels, local(): pl.pallas_call(functools.partial(gram_kernel, n), out_shape=jax.ShapeDtyp...  30.6 us
    mul x1, other arithmetic, local(): return (sums[0:1] * scale, sums[1:2] * scale, sums[2:3] * scale)  0.68 us

profile of v3, /device:TPU:19, one launch (start us, length us, event | category | flops | bytes accessed | tf_op | source)
XLA Modules:
  0.0 33.2 jit_solution(2925499463043799537)
XLA Ops:
  1.3 0.0 copy-start
  1.3 0.6 %copy-done = s32[1,2]{1,0:T(1,128)S(1)} copy-done((s32[1,2]{1,0:T(1,128)S(1)}, s32[1,2]{1,0:T(1,128)}, u32[]{:S(2)}) %copy-start) | copy-done | bytes 32
  1.9 30.6 %shard_map.67 = f32[3,128,128]{2,1,0:T(8,128)S(1)} custom-call(bf16[128,8192]{1,0:T(8,128)(2,1)} %in_hbm.1, bf16[128,8192]{1,0:T(8,128)(2,1)} %out_hbm.1, s32[1]{0:T(128)S(6)} %copy.7.counts_hbm, s32[2]{0:T(128)S(1)} %bitcast.1), custom_call_target="tpu_custom_call" | custom-call | tf_op jit(solution)/shard_map/pallas_call | solution.py:206
  32.6 0.7 %slice_multiply_fusion = (f32[1,128,128]{2,1,0:T(8,128)}, f32[1,128,128]{2,1,0:T(8,128)}, f32[1,128,128]{2,1,0:T(8,128)}) fusion(f32[3,128,128]{2,1,0:T(8,128)S(1)} %shard_map.67), kind=kLoop, calls=%fused_computation | loop fusion | flops 49152 | bytes 393216 | tf_op jit(solution)/shard_map/mul | solution.py:234
Async XLA Ops:
  1.3 0.7 %copy-start = (s32[1,2]{1,0:T(1,128)S(1)}, s32[1,2]{1,0:T(1,128)}, u32[]{:S(2)}) copy-start(s32[1,2]{1,0:T(1,128)} %param.7) | copy-start | bytes 28

commit v4 on v3

--- a/solution.py
+++ b/solution.py
@@ -118,13 +118,8 @@
         for i, values in enumerate(blocks(t * CLUSTER + q)):
             arrived[t, i, q] = values
 
-    def products(t):
-        left = arrived[t, 0].reshape(CLUSTER * rows, BS)
-        right = arrived[t, 1].reshape(CLUSTER * rows, BS)
-        target = arrived[t, 2].reshape(CLUSTER * rows, BS)
-        return (
-            contract_rows(left, right), contract_rows(left, target), contract_rows(target, target)
-        )
+    def held(t, i):
+        return arrived[t, i].reshape(CLUSTER * rows, BS)
 
     def tile_of(slot):
         right, left = span - 1 - z, z
@@ -152,10 +147,9 @@
         def _():
             send_raw(tile_of(slot + AHEAD))
 
-        for i, values in enumerate(products(t)):
-            partial[t, i] = values
-
-        for i in range(PARTS):
+        for i, (left, right) in enumerate(((0, 1), (0, 2), (2, 2))):
+            partial[t, i] = contract_rows(held(t, left), held(t, right))
+
             @pl.when((z > 0) & (t >= z))
             def _():
                 right_copy(t, i).wait_recv()
@@ -203,6 +197,10 @@
     half, full = span_inputs.dtype, jnp.float32
     scratch = 2 * (2 * rows * width + 2 * n * 3 * rows * BS) + 4 * 3 * span * 3 * BS * BS
     dma = pltpu.SemaphoreType.DMA
+    inputs, outputs, pairs = [
+        pltpu.with_memory_space_constraint(operand, pltpu.HBM)
+        for operand in (span_inputs, span_outputs, tile_pairs.reshape(2))
+    ]
     sums = pl.pallas_call(
         functools.partial(gram_kernel, n),
         out_shape=jax.ShapeDtypeStruct((3, BS, BS), full),
@@ -228,9 +226,9 @@
             *[dma((span, PARTS))] * 4,
         ],
         compiler_params=pltpu.CompilerParams(
-            collective_id=0, has_side_effects=True, vmem_limit_bytes=53 * 2**20
+            collective_id=0, has_side_effects=True, vmem_limit_bytes=scratch + 6 * 2**20
         ),
-    )(span_inputs, span_outputs, row_counts, tile_pairs.reshape(2))
+    )(inputs, outputs, row_counts, pairs)
     return (sums[0:1] * scale, sums[1:2] * scale, sums[2:3] * scale)
 
 

time: 33.4 us -> 32.7 us (0.979)
  local copies, waits for them, and re-layouts: 0.65 us -> 0 us
    unnamed x2 -> x0, local copies, waits for them, and re-layouts: 0.65 us -> none
where the time goes in v4:
time: 32.7 us; the launch traced here: 32.5 us
  Pallas kernels  30.5 us (93%)
  between operations  1.28 us (4%)
  other arithmetic  0.68 us (2%)
    pallas_call x1, Pallas kernels, local(): pl.pallas_call(functools.partial(gram_kernel, n), out_shape=jax.ShapeDtyp...  30.5 us
    mul x1, other arithmetic, local(): return (sums[0:1] * scale, sums[1:2] * scale, sums[2:3] * scale)  0.68 us

profile of v4, /device:TPU:19, one launch (start us, length us, event | category | flops | bytes accessed | tf_op | source)
XLA Modules:
  0.0 32.5 jit_solution(18325899241719826105)
XLA Ops:
  1.3 30.5 %shard_map.67 = f32[3,128,128]{2,1,0:T(8,128)S(1)} custom-call(bf16[128,8192]{1,0:T(8,128)(2,1)} %in_hbm.1, bf16[128,8192]{1,0:T(8,128)(2,1)} %out_hbm.1, s32[1]{0:T(128)S(6)} %copy.7.counts_hbm, s32[2]{0:T(128)} %bitcast.1), custom_call_target="tpu_custom_call" | custom-call | tf_op jit(solution)/shard_map/pallas_call | solution.py:204
  31.8 0.7 %slice_multiply_fusion = (f32[1,128,128]{2,1,0:T(8,128)}, f32[1,128,128]{2,1,0:T(8,128)}, f32[1,128,128]{2,1,0:T(8,128)}) fusion(f32[3,128,128]{2,1,0:T(8,128)S(1)} %shard_map.67), kind=kLoop, calls=%fused_computation | loop fusion | flops 49152 | bytes 393216 | tf_op jit(solution)/shard_map/mul | solution.py:232

commit v5 on v4

--- a/solution.py
+++ b/solution.py
@@ -10,7 +10,7 @@
 
 BS = 128
 CLUSTER = 4
-AHEAD = 2
+AHEAD = 3
 PARTS = 3
 
 
@@ -34,12 +34,13 @@
     load_pairs.start()
     load_counts.start()
 
+    turn = jnp.where(z < span // 2, n - 1, 1)
     barrier = pltpu.get_barrier_semaphore()
 
     @pl.loop(1, n)
     def _(step):
         pl.semaphore_signal(
-            barrier, inc=1, device_id={"rows": (me + step) % n}, device_id_type=pl.DeviceIdType.MESH
+            barrier, inc=1, device_id={"rows": (me + step * turn) % n}, device_id_type=pl.DeviceIdType.MESH
         )
 
     @pl.loop(0, in_v.shape[0])
@@ -57,8 +58,6 @@
             src_ref=pairs, dst_ref=all_pairs.at[slot], send_sem=pair_send.at[peer],
             recv_sem=pair_recv.at[slot], device_id={"rows": peer}, device_id_type=pl.DeviceIdType.MESH,
         )
-
-    turn = jnp.where(z < span // 2, n - 1, 1)
 
     @pl.loop(1, n)
     def _(step):
@@ -143,30 +142,30 @@
             source = (q + offset) % CLUSTER
             raw_copy(t, source, source).wait_recv()
 
+        for i, (left, right) in enumerate(((0, 1), (0, 2), (2, 2))):
+            partial[t, i] = contract_rows(held(t, left), held(t, right))
+
+            @pl.when((z > 0) & (t >= z))
+            def _():
+                right_copy(t, i).wait_recv()
+                partial[t, i] = partial[t, i] + from_left[t, i]
+
+            @pl.when((z < span - 1) & (t <= z))
+            def _():
+                left_copy(t, i).wait_recv()
+                partial[t, i] = partial[t, i] + from_right[t, i]
+
+            @pl.when(t > z)
+            def _():
+                right_copy(t, i).start()
+
+            @pl.when(t < z)
+            def _():
+                left_copy(t, i).start()
+
         @pl.when(slot + AHEAD < span)
         def _():
             send_raw(tile_of(slot + AHEAD))
-
-        for i, (left, right) in enumerate(((0, 1), (0, 2), (2, 2))):
-            partial[t, i] = contract_rows(held(t, left), held(t, right))
-
-            @pl.when((z > 0) & (t >= z))
-            def _():
-                right_copy(t, i).wait_recv()
-                partial[t, i] = partial[t, i] + from_left[t, i]
-
-            @pl.when((z < span - 1) & (t <= z))
-            def _():
-                left_copy(t, i).wait_recv()
-                partial[t, i] = partial[t, i] + from_right[t, i]
-
-            @pl.when(t > z)
-            def _():
-                right_copy(t, i).start()
-
-            @pl.when(t < z)
-            def _():
-                left_copy(t, i).start()
 
     sums_ref[...] = partial[z]
 

time: 32.7 us -> 32.5 us (level)
  no operation moved by 1% of the time
where the time goes in v5:
time: 32.5 us; the launch traced here: 32.3 us
  Pallas kernels  30.3 us (93%)
  between operations  1.28 us (4%)
  other arithmetic  0.68 us (2%)
    pallas_call x1, Pallas kernels, local(): pl.pallas_call(functools.partial(gram_kernel, n), out_shape=jax.ShapeDtyp...  30.3 us
    mul x1, other arithmetic, local(): return (sums[0:1] * scale, sums[1:2] * scale, sums[2:3] * scale)  0.68 us

profile of v5, /device:TPU:19, one launch (start us, length us, event | category | flops | bytes accessed | tf_op | source)
XLA Modules:
  0.0 32.3 jit_solution(17892727584191631841)
XLA Ops:
  1.3 30.3 %shard_map.67 = f32[3,128,128]{2,1,0:T(8,128)S(1)} custom-call(bf16[128,8192]{1,0:T(8,128)(2,1)} %in_hbm.1, bf16[128,8192]{1,0:T(8,128)(2,1)} %out_hbm.1, s32[1]{0:T(128)S(6)} %copy.7.counts_hbm, s32[2]{0:T(128)} %bitcast.1), custom_call_target="tpu_custom_call" | custom-call | tf_op jit(solution)/shard_map/pallas_call | solution.py:203
  31.6 0.7 %slice_multiply_fusion = (f32[1,128,128]{2,1,0:T(8,128)}, f32[1,128,128]{2,1,0:T(8,128)}, f32[1,128,128]{2,1,0:T(8,128)}) fusion(f32[3,128,128]{2,1,0:T(8,128)S(1)} %shard_map.67), kind=kLoop, calls=%fused_computation | loop fusion | flops 49152 | bytes 393216 | tf_op jit(solution)/shard_map/mul | solution.py:231

commit v6 on v5

--- a/solution.py
+++ b/solution.py
@@ -11,7 +11,7 @@
 BS = 128
 CLUSTER = 4
 AHEAD = 3
-PARTS = 3
+PARTS = 2
 
 
 def contract_rows(left, right):
@@ -86,16 +86,19 @@
             device_id={"rows": z * CLUSTER + dest}, device_id_type=pl.DeviceIdType.MESH,
         )
 
+    def group(i):
+        return pl.ds(i, i + 1)
+
     def right_copy(t, i):
         return pltpu.make_async_remote_copy(
-            src_ref=partial.at[t, i], dst_ref=from_left.at[t, i], send_sem=right_send.at[t, i],
+            src_ref=partial.at[t, group(i)], dst_ref=from_left.at[t, group(i)], send_sem=right_send.at[t, i],
             recv_sem=right_recv.at[t, i], device_id={"rows": (me + CLUSTER) % n},
             device_id_type=pl.DeviceIdType.MESH,
         )
 
     def left_copy(t, i):
         return pltpu.make_async_remote_copy(
-            src_ref=partial.at[t, i], dst_ref=from_right.at[t, i], send_sem=left_send.at[t, i],
+            src_ref=partial.at[t, group(i)], dst_ref=from_right.at[t, group(i)], send_sem=left_send.at[t, i],
             recv_sem=left_recv.at[t, i], device_id={"rows": (me + n - CLUSTER) % n},
             device_id_type=pl.DeviceIdType.MESH,
         )
@@ -142,18 +145,19 @@
             source = (q + offset) % CLUSTER
             raw_copy(t, source, source).wait_recv()
 
-        for i, (left, right) in enumerate(((0, 1), (0, 2), (2, 2))):
-            partial[t, i] = contract_rows(held(t, left), held(t, right))
+        for i in range(PARTS):
+            for j, left, right in (((0, 0, 1),), ((1, 0, 2), (2, 2, 2)))[i]:
+                partial[t, j] = contract_rows(held(t, left), held(t, right))
 
             @pl.when((z > 0) & (t >= z))
             def _():
                 right_copy(t, i).wait_recv()
-                partial[t, i] = partial[t, i] + from_left[t, i]
+                partial[t, group(i)] = partial[t, group(i)] + from_left[t, group(i)]
 
             @pl.when((z < span - 1) & (t <= z))
             def _():
                 left_copy(t, i).wait_recv()
-                partial[t, i] = partial[t, i] + from_right[t, i]
+                partial[t, group(i)] = partial[t, group(i)] + from_right[t, group(i)]
 
             @pl.when(t > z)
             def _():

time: 32.5 us -> 34.2 us (1.052)
  the two profiles are of different devices: /device:TPU:19 before, /device:TPU:0 now
where the time goes in v6:
time: 34.2 us; the launch traced here: 34 us
  Pallas kernels  32.1 us (94%)
  between operations  1.28 us (4%)
  other arithmetic  0.68 us (2%)
    pallas_call x1, Pallas kernels, local(): pl.pallas_call(functools.partial(gram_kernel, n), out_shape=jax.ShapeDtyp...  32.1 us

profile of v6, /device:TPU:0, one launch (start us, length us, event | category | flops | bytes accessed | tf_op | source)
XLA Modules:
  0.0 34.0 jit_solution(9322923853688650192)
XLA Ops:
  1.3 32.1 %shard_map.67 = f32[3,128,128]{2,1,0:T(8,128)S(1)} custom-call(bf16[128,8192]{1,0:T(8,128)(2,1)} %in_hbm.1, bf16[128,8192]{1,0:T(8,128)(2,1)} %out_hbm.1, s32[1]{0:T(128)S(6)} %copy.7.counts_hbm, s32[2]{0:T(128)} %bitcast.1), custom_call_target="tpu_custom_call" | custom-call | tf_op jit(solution)/shard_map/pallas_call | solution.py:207
  33.3 0.7 %slice_multiply_fusion = (f32[1,128,128]{2,1,0:T(8,128)}, f32[1,128,128]{2,1,0:T(8,128)}, f32[1,128,128]{2,1,0:T(8,128)}) fusion(f32[3,128,128]{2,1,0:T(8,128)S(1)} %shard_map.67), kind=kLoop, calls=%fused_computation | loop fusion | flops 49152 | bytes 393216 | tf_op jit(solution)/shard_map/mul | solution.py:235
